TPU v7x, 512 devices: a whole 4x4x16 slice. The times are simulated.
512 devices in a mesh: grp: 8 (over y, core), mem: 64 (over x, z).
Axes of the slice: x: 4, y: 4, z: 16, core: 2. Of those that a mesh axis runs over, the one named last changes fastest.
Arguments:
- tokens: bfloat16 [65536, 1024], P(('grp', 'mem')), may hold values from -6 to 6
- cotangent: bfloat16 [65536, 1024], P(('grp', 'mem')), may hold values from -6 to 6
- path: int32 [512, 3], P(('grp', 'mem')), may hold values from 0 to 1023, as said below
- coarse_weights: bfloat16 [4, 1024, 512], P(None, 'mem'), may hold values from -0.1875 to 0.1875
- middle_weights: bfloat16 [64, 1024, 256], P(None, 'mem'), may hold values from -0.1875 to 0.1875
- fine_weights: bfloat16 [1024, 1024, 128], P('grp', 'mem'), may hold values from -0.1875 to 0.1875
Outputs:
- tokens_grad: bfloat16 [65536, 1024], P(('grp', 'mem'))
- coarse_grad: bfloat16 [4, 1024, 512], P(None, 'mem')
- middle_grad: bfloat16 [64, 1024, 256], P(None, 'mem')
- fine_grad: bfloat16 [1024, 1024, 128], P('grp', 'mem')
Inputs may be any that keep to these rules, and one draw needn't show every extreme that they name: Row d is the path of document d: column 0 its coarse block, column 1 its middle block, column 2 its fine block, with middle = fine * 64 // 1024 and coarse = middle * 4 // 64. Some fine blocks are chosen by many documents.
All inputs are finite; a program needn't handle non-finite values.
Results may differ from a plain program's by a relative error of at most 0.005.
Values may be sent and summed in bfloat16 or wider, within the bound.
No kernel may reach another device: no remote copies, remote signals or barrier semaphores. Data moves between devices by JAX's collectives and lax.ppermute only.
A program may use at most 64 MiB of HBM per device.

v0:
```python
from functools import partial
import jax
import jax.numpy as jnp
from jax import lax
from jax.sharding import PartitionSpec as P


def contract_rows(left, right):
    return lax.dot_general(
        left, right, (((0,), (0,)), ((), ())), preferred_element_type=jnp.float32
    )


def level_terms(inputs, upstream, weights):
    hidden_width = weights.shape[1] // 2
    up_half = weights[:, :hidden_width]
    down_half = weights[:, hidden_width:]
    before = jnp.dot(inputs, up_half, preferred_element_type=jnp.float32)
    hidden, pullback = jax.vjp(partial(jax.nn.gelu, approximate=True), before)
    hidden_low = hidden.astype(jnp.bfloat16)
    hidden_grad = jnp.dot(upstream, down_half, preferred_element_type=jnp.float32)
    before_grad = pullback(hidden_grad)[0].astype(jnp.bfloat16)
    up_grad = contract_rows(inputs, before_grad)
    down_grad = contract_rows(upstream, hidden_low)
    input_part = lax.dot_general(
        before_grad, up_half, (((1,), (1,)), ((), ())), preferred_element_type=jnp.float32
    )
    return (jnp.concatenate([up_grad, down_grad], axis=1), input_part)


def one_hot_rows(identity, count):
    return (identity[:, None] == jnp.arange(count, dtype=jnp.int32)[None, :]).astype(jnp.bfloat16)


def select_blocks(picker, blocks):
    return jnp.einsum("mk,krh->mrh", picker, blocks, preferred_element_type=jnp.float32).astype(
        jnp.bfloat16
    )


def collect_blocks(picker, pieces):
    return jnp.einsum(
        "mk,mrh->krh", picker.astype(jnp.float32), pieces, precision=lax.Precision.HIGHEST
    )


def on_device(tokens, cotangent, path, coarse_weights, middle_weights, fine_weights):
    member_count = lax.axis_size("mem")
    group_count = lax.axis_size("grp")
    group = lax.axis_index("grp")
    row_count = coarse_weights.shape[1]
    fine_owned = fine_weights.shape[0]
    route = path[0]
    all_paths = lax.all_gather(path, ("grp", "mem"), axis=0, tiled=True)
    group_paths = lax.dynamic_slice_in_dim(all_paths, group * member_count, member_count, 0)
    coarse_pick = one_hot_rows(group_paths[:, 0], coarse_weights.shape[0])
    middle_pick = one_hot_rows(group_paths[:, 1], middle_weights.shape[0])
    middle_send = select_blocks(middle_pick, middle_weights)
    every_block = lax.all_gather(coarse_weights, "mem", axis=1, tiled=True)
    coarse_block = lax.dynamic_index_in_dim(every_block, route[0], 0, keepdims=False)
    middle_block = lax.all_to_all(middle_send, "mem", split_axis=0, concat_axis=1, tiled=True)[0]
    offsets = all_paths[:, 2] - group * fine_owned
    fine_pick = one_hot_rows(offsets, fine_owned)
    fine_send = select_blocks(fine_pick, fine_weights).reshape(
        group_count, member_count, row_count, fine_weights.shape[2]
    )
    arrived = lax.all_to_all(fine_send, "grp", split_axis=0, concat_axis=0, tiled=True)
    merged = jnp.sum(arrived, axis=0, dtype=jnp.float32).astype(jnp.bfloat16)
    fine_block = lax.all_to_all(merged, "mem", split_axis=0, concat_axis=1, tiled=True)[0]
    coarse_term, coarse_back = level_terms(tokens, cotangent, coarse_block)
    middle_term, middle_back = level_terms(tokens, cotangent, middle_block)
    fine_term, fine_back = level_terms(tokens, cotangent, fine_block)
    tokens_grad = (coarse_back + middle_back + fine_back).astype(jnp.bfloat16)
    coarse_parts, middle_parts = (
        lax.all_to_all(
            coarse_term.reshape(member_count, row_count, -1),
            "mem",
            split_axis=0,
            concat_axis=0,
            tiled=True,
        ),
        lax.all_to_all(
            middle_term.reshape(member_count, row_count, -1),
            "mem",
            split_axis=0,
            concat_axis=0,
            tiled=True,
        ),
    )
    coarse_local = collect_blocks(coarse_pick, coarse_parts)
    middle_local = collect_blocks(middle_pick, middle_parts)
    coarse_total, middle_total = lax.psum((coarse_local, middle_local), "grp")
    fine_parts = lax.all_to_all(
        fine_term.reshape(member_count, row_count, -1),
        "mem",
        split_axis=0,
        concat_axis=0,
        tiled=True,
    )
    owner_group = group_paths[:, 2] // fine_owned
    destined = (jnp.arange(group_count, dtype=jnp.int32)[:, None] == owner_group[None, :]).astype(
        jnp.float32
    )
    outgoing = destined[:, :, None, None] * fine_parts[None]
    returned = lax.all_to_all(outgoing, "grp", split_axis=0, concat_axis=0, tiled=True)
    fine_local = collect_blocks(
        fine_pick, returned.reshape(group_count * member_count, row_count, -1)
    )
    return (
        tokens_grad,
        coarse_total.astype(jnp.bfloat16),
        middle_total.astype(jnp.bfloat16),
        fine_local.astype(jnp.bfloat16),
    )


def solution(mesh):
    return jax.shard_map(
        on_device,
        mesh=mesh,
        in_specs=(
            P(("grp", "mem"), None),
            P(("grp", "mem"), None),
            P(("grp", "mem"), None),
            P(None, "mem", None),
            P(None, "mem", None),
            P("grp", "mem", None),
        ),
        out_specs=(
            P(("grp", "mem"), None),
            P(None, "mem", None),
            P(None, "mem", None),
            P("grp", "mem", None),
        ),
        check_vma=False,
    )
```

profile of v0, /device:TPU:63, one launch (start us, length us, event | category | flops | bytes accessed | tf_op | source)
XLA Modules:
  0.0 555.5 jit_solution(7141725121758117286)
XLA Ops:
  7.2 104.7 %all-gather = s32[512,1,3]{2,1,0:T(1,128)S(1)} all-gather(s32[1,1,3]{2,1,0:T(1,128)} %bitcast.100), channel_id=1, replica_groups=mesh['grp'=8,'mem'=64] {'grp','mem'}, dimensions={0}, use_global_device_ids=true | all-gather | bytes 6156 | tf_op jit(solution)/shard_map/all_gather | solution.py:54
  113.2 32.7 %all_to_all.43 = bf16[8,64,16,128]{3,1,2,0:T(8,128)(2,1)S(1)} all-to-all(bf16[8,64,16,128]{3,1,2,0:T(8,128)(2,1)S(1)} %copy.78), channel_id=1, replica_groups=mesh['grp'=8,'mem'=64] {'grp'}, dimensions={0} | all-to-all | bytes 4194304 | tf_op jit(solution)/shard_map/all_to_all | solution.py:67
  146.2 0.9 copy.80
  147.1 12.7 %all-to-all-start.2 = ((bf16[64,16,128]{2,1,0:T(8,128)(2,1)}), bf16[64,16,128]{2,1,0:T(8,128)(2,1)S(1)}, u32[]{:S(2)}, u32[]{:S(2)}) async-start(bf16[64,16,128]{2,1,0:T(8,128)(2,1)} %copy.80), calls=%async_computation.2 | async-start | bytes 524288 | tf_op jit(solution)/shard_map/all_to_all | solution.py:69
  159.9 1.4 convolution_convert_fusion.1
  161.3 1.1 copy.75
  162.4 16.9 %all-to-all-done.2 = bf16[64,16,128]{2,1,0:T(8,128)(2,1)S(1)} async-done(((bf16[64,16,128]{2,1,0:T(8,128)(2,1)}), bf16[64,16,128]{2,1,0:T(8,128)(2,1)S(1)}, u32[]{:S(2)}, u32[]{:S(2)}) %all-to-all-start.2) | async-done | bytes 262176 | tf_op jit(solution)/shard_map/all_to_all | solution.py:69
  179.3 7.3 %all-to-all-start = ((bf16[64,16,256]{2,1,0:T(8,128)(2,1)}), bf16[64,16,256]{2,1,0:T(8,128)(2,1)S(1)}, u32[]{:S(2)}, u32[]{:S(2)}) async-start(bf16[64,16,256]{2,1,0:T(8,128)(2,1)} %copy.75), calls=%async_computation | async-start | bytes 1048576 | tf_op jit(solution)/shard_map/all_to_all | solution.py:61
  187.6 1.0 copy.85
  188.6 28.1 %all-to-all-done = bf16[64,16,256]{2,1,0:T(8,128)(2,1)S(1)} async-done(((bf16[64,16,256]{2,1,0:T(8,128)(2,1)}), bf16[64,16,256]{2,1,0:T(8,128)(2,1)S(1)}, u32[]{:S(2)}, u32[]{:S(2)}) %all-to-all-start) | async-done | bytes 524320 | tf_op jit(solution)/shard_map/all_to_all | solution.py:61
  216.7 8.0 %all-to-all-start.5 = ((f32[64,16,128]{2,1,0:T(8,128)}), f32[64,16,128]{2,1,0:T(8,128)}, u32[]{:S(2)}, u32[]{:S(2)}) async-start(f32[64,16,128]{2,1,0:T(8,128)} %bitcast.30), calls=%async_computation.5 | async-start | bytes 1048576 | tf_op jit(solution)/shard_map/all_to_all | solution.py:93
  226.6 1.3 copy.83
  228.0 28.1 %all-to-all-done.5 = f32[64,16,128]{2,1,0:T(8,128)} async-done(((f32[64,16,128]{2,1,0:T(8,128)}), f32[64,16,128]{2,1,0:T(8,128)}, u32[]{:S(2)}, u32[]{:S(2)}) %all-to-all-start.5) | async-done | bytes 524320 | tf_op jit(solution)/shard_map/all_to_all | solution.py:93
  256.0 6.6 %all-to-all-start.4 = ((f32[64,16,256]{2,1,0:T(8,128)}), f32[64,16,256]{2,1,0:T(8,128)S(1)}, u32[]{:S(2)}, u32[]{:S(2)}) async-start(f32[64,16,256]{2,1,0:T(8,128)} %bitcast.25), calls=%async_computation.4 | async-start | bytes 2097152 | tf_op jit(solution)/shard_map/all_to_all | solution.py:82
  262.7 1.2 copy.86
  263.9 2.6 broadcast_multiply_fusion
  266.5 51.7 %all-to-all-done.4 = f32[64,16,256]{2,1,0:T(8,128)S(1)} async-done(((f32[64,16,256]{2,1,0:T(8,128)}), f32[64,16,256]{2,1,0:T(8,128)S(1)}, u32[]{:S(2)}, u32[]{:S(2)}) %all-to-all-start.4) | async-done | bytes 1048608 | tf_op jit(solution)/shard_map/all_to_all | solution.py:82
  318.2 1.0 copy-done.2
  319.2 9.0 %all-to-all-start.6 = ((f32[8,64,16,128]{3,1,2,0:T(8,128)}), f32[8,64,16,128]{3,1,2,0:T(8,128)}, u32[]{:S(2)}, u32[]{:S(2)}) async-start(f32[8,64,16,128]{3,1,2,0:T(8,128)} %broadcast_multiply_fusion), calls=%async_computation.6 | async-start | bytes 8388608 | tf_op jit(solution)/shard_map/all_to_all | solution.py:105
  328.4 50.9 %all-gather.3.cloned.1.call-done = bf16[4,1024,512]{2,1,0:T(8,128)(2,1)} async-done(((bf16[4,16,512]{2,1,0:T(8,128)(2,1)}), bf16[4,1024,512]{2,1,0:T(8,128)(2,1)}) %all-gather.3.cloned.1.call-update) | async-done | bytes 4194320 | tf_op jit(solution)/shard_map/all_gather | solution.py:59
  379.3 1.3 dynamic-slice_bitcast_fusion
  382.0 1.9 copy.81
  383.9 10.2 %all-to-all-start.3 = ((f32[64,16,512]{2,1,0:T(8,128)}), f32[64,16,512]{2,1,0:T(8,128)S(1)}, u32[]{:S(2)}, u32[]{:S(2)}) async-start(f32[64,16,512]{2,1,0:T(8,128)} %bitcast.89), calls=%async_computation.3 | async-start | bytes 4194304 | tf_op jit(solution)/shard_map/all_to_all | solution.py:75
  394.1 3.6 fusion.3
  398.3 1.0 fusion.2
  399.3 2.5 copy.87
  401.8 1.7 convolution_convert_fusion.2
  403.5 1.1 copy.90
  404.6 81.4 %all-to-all-done.3 = f32[64,16,512]{2,1,0:T(8,128)S(1)} async-done(((f32[64,16,512]{2,1,0:T(8,128)}), f32[64,16,512]{2,1,0:T(8,128)S(1)}, u32[]{:S(2)}, u32[]{:S(2)}) %all-to-all-start.3) | async-done | bytes 2097184 | tf_op jit(solution)/shard_map/all_to_all | solution.py:75
  486.0 2.0 fusion
  488.0 59.0 %all-reduce.2 = (bf16[4,16,512]{2,0,1:T(4,128)(2,1)S(1)}, bf16[64,16,256]{2,0,1:T(8,128)(2,1)S(1)}) all-reduce(f32[4,16,512]{2,0,1:T(4,128)S(1)} %fusion, f32[64,16,256]{2,0,1:T(8,128)} %fusion.3), channel_id=1, replica_groups=mesh['grp'=8,'mem'=64] {'grp'}, use_global_device_ids=true, to_apply=%region_1.2 | all-reduce | flops 294912 | bytes 1769472 | tf_op jit(solution)/shard_map/psum | solution.py:92
  547.6 1.1 copy.89
  (47 shorter events, 7.1 us)
Async XLA Ops:
  7.2 105.0 %copy-start = (bf16[128,16,128]{2,1,0:T(8,128)(2,1)S(1)}, bf16[128,16,128]{2,1,0:T(8,128)(2,1)}, u32[]{:S(2)}) copy-start(bf16[128,16,128]{2,1,0:T(8,128)(2,1)} %param.11) | copy-start | bytes 1572868
  146.2 40.4 %copy-start.1 = (bf16[128,1024]{1,0:T(8,128)(2,1)S(1)}, bf16[128,1024]{1,0:T(8,128)(2,1)}, u32[]{:S(2)}) copy-start(bf16[128,1024]{1,0:T(8,128)(2,1)} %param.6) | copy-start | bytes 786436
  147.1 39.8 %copy-start.5 = (bf16[128,1024]{1,0:T(8,128)(2,1)S(1)}, bf16[128,1024]{1,0:T(8,128)(2,1)}, u32[]{:S(2)}) copy-start(bf16[128,1024]{1,0:T(8,128)(2,1)} %param.7) | copy-start | bytes 786436
  147.1 32.2 %all-to-all-start.2 = ((bf16[64,16,128]{2,1,0:T(8,128)(2,1)}), bf16[64,16,128]{2,1,0:T(8,128)(2,1)S(1)}, u32[]{:S(2)}, u32[]{:S(2)}) async-start(bf16[64,16,128]{2,1,0:T(8,128)(2,1)} %copy.80), calls=%async_computation.2 | async-start | bytes 524288 | tf_op jit(solution)/shard_map/all_to_all | solution.py:69
  179.3 37.4 %all-to-all-start = ((bf16[64,16,256]{2,1,0:T(8,128)(2,1)}), bf16[64,16,256]{2,1,0:T(8,128)(2,1)S(1)}, u32[]{:S(2)}, u32[]{:S(2)}) async-start(bf16[64,16,256]{2,1,0:T(8,128)(2,1)} %copy.75), calls=%async_computation | async-start | bytes 1048576 | tf_op jit(solution)/shard_map/all_to_all | solution.py:61
  216.7 9.8 %copy-start.6 = (bf16[64,16,256]{2,1,0:T(8,128)(2,1)}, bf16[64,16,256]{2,1,0:T(8,128)(2,1)S(1)}, u32[]{:S(2)}) copy-start(bf16[64,16,256]{2,1,0:T(8,128)(2,1)S(1)} %all-to-all-done) | copy-start | bytes 1572868
  216.7 39.3 %all-to-all-start.5 = ((f32[64,16,128]{2,1,0:T(8,128)}), f32[64,16,128]{2,1,0:T(8,128)}, u32[]{:S(2)}, u32[]{:S(2)}) async-start(f32[64,16,128]{2,1,0:T(8,128)} %bitcast.30), calls=%async_computation.5 | async-start | bytes 1048576 | tf_op jit(solution)/shard_map/all_to_all | solution.py:93
  224.8 154.5 %all-gather.3.cloned.1.call-start = ((), (), s32[]{:S(2)}) async-start(), calls=%async_computation.7 | async-start | bytes 4259840 | tf_op jit(solution)/shard_map/all_gather | solution.py:59
  256.0 62.2 %all-to-all-start.4 = ((f32[64,16,256]{2,1,0:T(8,128)}), f32[64,16,256]{2,1,0:T(8,128)S(1)}, u32[]{:S(2)}, u32[]{:S(2)}) async-start(f32[64,16,256]{2,1,0:T(8,128)} %bitcast.25), calls=%async_computation.4 | async-start | bytes 2097152 | tf_op jit(solution)/shard_map/all_to_all | solution.py:82
  266.5 61.8 %copy-start.8 = (s32[1,3]{1,0:T(1,128)S(1)}, s32[1,3]{1,0:T(1,128)}, u32[]{:S(2)}) copy-start(s32[1,3]{1,0:T(1,128)} %param.8) | copy-start | bytes 40
  318.2 1.0 copy-start.2
  319.2 64.7 %all-to-all-start.6 = ((f32[8,64,16,128]{3,1,2,0:T(8,128)}), f32[8,64,16,128]{3,1,2,0:T(8,128)}, u32[]{:S(2)}, u32[]{:S(2)}) async-start(f32[8,64,16,128]{3,1,2,0:T(8,128)} %broadcast_multiply_fusion), calls=%async_computation.6 | async-start | bytes 8388608 | tf_op jit(solution)/shard_map/all_to_all | solution.py:105
  380.6 1.0 copy-start.3
  383.9 102.1 %all-to-all-start.3 = ((f32[64,16,512]{2,1,0:T(8,128)}), f32[64,16,512]{2,1,0:T(8,128)S(1)}, u32[]{:S(2)}, u32[]{:S(2)}) async-start(f32[64,16,512]{2,1,0:T(8,128)} %bitcast.89), calls=%async_computation.3 | async-start | bytes 4194304 | tf_op jit(solution)/shard_map/all_to_all | solution.py:75
  394.1 3.6 copy-start.4
  394.1 4.0 copy-start.7
Sparse Core Ops, SparseCore 0:
  228.6 150.6 all-gather.2
where the time goes:
time: 556 us
  waiting for transfers between devices  258 us (46%)
  blocking collectives  196 us (35%)
  starting transfers between devices  53.9 us (10%)
  local copies, waits for them, and re-layouts  15.4 us (3%)
  between operations  14.5 us (3%)
  matrix products  14.1 us (3%)
    all_gather x1, blocking collectives, on_device(): all_paths = lax.all_gather(path, ('grp', 'mem'), axis=0, tiled=True)  105 us
    all_to_all x1, waiting for transfers between devices, on_device(): lax.all_to_all(coarse_term.reshape(member_count, row_count, -1), 'mem', s...  81.4 us
    psum x1, blocking collectives, on_device(): coarse_total, middle_total = lax.psum((coarse_local, middle_local), 'grp')  59 us
    all_to_all x1, waiting for transfers between devices, on_device(): lax.all_to_all(middle_term.reshape(member_count, row_count, -1), 'mem', s...  51.7 us
    all_gather x1, waiting for transfers between devices, on_device(): every_block = lax.all_gather(coarse_weights, 'mem', axis=1, tiled=True)  50.9 us
    all_to_all x1, blocking collectives, on_device(): lax.all_to_all(fine_send, 'grp', split_axis=0, concat_axis=0, tiled=True)  32.7 us
    all_to_all x1, waiting for transfers between devices, on_device(): lax.all_to_all(middle_send, 'mem', split_axis=0, concat_axis=1, tiled=True)  28.1 us
    all_to_all x1, waiting for transfers between devices, on_device(): lax.all_to_all(fine_term.reshape(member_count, row_count, -1), 'mem', spl...  28.1 us
  transfers between devices with their start and end apart: 7, of which 6 were waited for; matrix products, arithmetic and copies ran while one was open for 5% of the time, Pallas kernels for 0%

commit v1 on v0

--- a/solution.py
+++ b/solution.py
@@ -3,6 +3,14 @@
 import jax.numpy as jnp
 from jax import lax
 from jax.sharding import PartitionSpec as P
+
+
+def tiled_gather(shard, axis, dim):
+    peers = lax.axis_size(axis)
+    repeats = [peers if d == dim else 1 for d in range(shard.ndim)]
+    return lax.all_to_all(
+        jnp.tile(shard, repeats), axis, split_axis=dim, concat_axis=dim, tiled=True
+    )
 
 
 def contract_rows(left, right):
@@ -56,7 +64,7 @@
     coarse_pick = one_hot_rows(group_paths[:, 0], coarse_weights.shape[0])
     middle_pick = one_hot_rows(group_paths[:, 1], middle_weights.shape[0])
     middle_send = select_blocks(middle_pick, middle_weights)
-    every_block = lax.all_gather(coarse_weights, "mem", axis=1, tiled=True)
+    every_block = tiled_gather(coarse_weights, "mem", 1)
     coarse_block = lax.dynamic_index_in_dim(every_block, route[0], 0, keepdims=False)
     middle_block = lax.all_to_all(middle_send, "mem", split_axis=0, concat_axis=1, tiled=True)[0]
     offsets = all_paths[:, 2] - group * fine_owned

time: 556 us -> 727 us (1.31)
  the two profiles are of different devices: /device:TPU:63 before, /device:TPU:31 now
where the time goes in v1:
time: 727 us; the launch traced here: 726 us
  waiting for transfers between devices  415 us (57%)
  blocking collectives  200 us (28%)
  starting transfers between devices  70.4 us (10%)
  local copies, waits for them, and re-layouts  21.8 us (3%)
  matrix products  13.9 us (2%)
    all_to_all x1, waiting for transfers between devices, tiled_gather(): lax.all_to_all(jnp.tile(shard, repeats), axis, split_axis=dim, concat_axi...  177 us
    all_gather x1, blocking collectives, on_device(): all_paths = lax.all_gather(path, ('grp', 'mem'), axis=0, tiled=True)  105 us
    all_to_all x1, waiting for transfers between devices, on_device(): lax.all_to_all(coarse_term.reshape(member_count, row_count, -1), 'mem', s...  80.5 us
    psum x1, blocking collectives, on_device(): coarse_total, middle_total = lax.psum((coarse_local, middle_local), 'grp')  60.9 us
    all_to_all x1, waiting for transfers between devices, on_device(): lax.all_to_all(middle_term.reshape(member_count, row_count, -1), 'mem', s...  50 us
    all_to_all x1, waiting for transfers between devices, on_device(): lax.all_to_all(outgoing, 'grp', split_axis=0, concat_axis=0, tiled=True)  39.1 us
    all_to_all x1, blocking collectives, on_device(): lax.all_to_all(fine_send, 'grp', split_axis=0, concat_axis=0, tiled=True)  34 us
    all_to_all x1, waiting for transfers between devices, on_device(): lax.all_to_all(fine_term.reshape(member_count, row_count, -1), 'mem', spl...  26.6 us
  transfers between devices with their start and end apart: 7, of which 7 were waited for; matrix products, arithmetic and copies ran while one was open for 4% of the time, Pallas kernels for 0%

profile of v1, /device:TPU:31, one launch (start us, length us, event | category | flops | bytes accessed | tf_op | source)
XLA Modules:
  0.0 726.1 jit_solution(5686502105720229815)
XLA Ops:
  0.6 105.3 %all-gather = s32[512,1,3]{2,1,0:T(1,128)S(1)} all-gather(s32[1,1,3]{2,1,0:T(1,128)} %bitcast.106), channel_id=1, replica_groups=mesh['grp'=8,'mem'=64] {'grp','mem'}, dimensions={0}, use_global_device_ids=true | all-gather | bytes 6156 | tf_op jit(solution)/shard_map/all_gather | solution.py:62
  107.2 34.0 %all_to_all.48 = bf16[8,64,16,128]{3,1,2,0:T(8,128)(2,1)S(1)} all-to-all(bf16[8,64,16,128]{3,1,2,0:T(8,128)(2,1)S(1)} %copy.83), channel_id=1, replica_groups=mesh['grp'=8,'mem'=64] {'grp'}, dimensions={0} | all-to-all | bytes 4194304 | tf_op jit(solution)/shard_map/all_to_all | solution.py:75
  142.5 11.3 %all-to-all-start.3 = ((bf16[64,16,128]{2,1,0:T(8,128)(2,1)}), bf16[64,16,128]{2,1,0:T(8,128)(2,1)S(1)}, u32[]{:S(2)}, u32[]{:S(2)}) async-start(bf16[64,16,128]{2,1,0:T(8,128)(2,1)} %copy.85), calls=%async_computation.3 | async-start | bytes 524288 | tf_op jit(solution)/shard_map/all_to_all | solution.py:77
  153.8 1.4 convolution_convert_fusion.1
  155.3 1.1 copy.80
  156.3 16.3 %all-to-all-done.3 = bf16[64,16,128]{2,1,0:T(8,128)(2,1)S(1)} async-done(((bf16[64,16,128]{2,1,0:T(8,128)(2,1)}), bf16[64,16,128]{2,1,0:T(8,128)(2,1)S(1)}, u32[]{:S(2)}, u32[]{:S(2)}) %all-to-all-start.3) | async-done | bytes 262176 | tf_op jit(solution)/shard_map/all_to_all | solution.py:77
  172.6 7.9 %all-to-all-start.1 = ((bf16[64,16,256]{2,1,0:T(8,128)(2,1)}), bf16[64,16,256]{2,1,0:T(8,128)(2,1)S(1)}, u32[]{:S(2)}, u32[]{:S(2)}) async-start(bf16[64,16,256]{2,1,0:T(8,128)(2,1)} %copy.80), calls=%async_computation.1 | async-start | bytes 1048576 | tf_op jit(solution)/shard_map/all_to_all | solution.py:69
  181.5 1.0 copy.90
  182.5 26.3 %all-to-all-done.1 = bf16[64,16,256]{2,1,0:T(8,128)(2,1)S(1)} async-done(((bf16[64,16,256]{2,1,0:T(8,128)(2,1)}), bf16[64,16,256]{2,1,0:T(8,128)(2,1)S(1)}, u32[]{:S(2)}, u32[]{:S(2)}) %all-to-all-start.1) | async-done | bytes 524320 | tf_op jit(solution)/shard_map/all_to_all | solution.py:69
  208.9 9.8 %all-to-all-start.6 = ((f32[64,16,128]{2,1,0:T(8,128)}), f32[64,16,128]{2,1,0:T(8,128)}, u32[]{:S(2)}, u32[]{:S(2)}) async-start(f32[64,16,128]{2,1,0:T(8,128)} %bitcast.31), calls=%async_computation.6 | async-start | bytes 1048576 | tf_op jit(solution)/shard_map/all_to_all | solution.py:101
  219.8 1.3 copy.88
  221.1 26.6 %all-to-all-done.6 = f32[64,16,128]{2,1,0:T(8,128)} async-done(((f32[64,16,128]{2,1,0:T(8,128)}), f32[64,16,128]{2,1,0:T(8,128)}, u32[]{:S(2)}, u32[]{:S(2)}) %all-to-all-start.6) | async-done | bytes 524320 | tf_op jit(solution)/shard_map/all_to_all | solution.py:101
  247.7 8.9 %all-to-all-start.5 = ((f32[64,16,256]{2,1,0:T(8,128)}), f32[64,16,256]{2,1,0:T(8,128)S(1)}, u32[]{:S(2)}, u32[]{:S(2)}) async-start(f32[64,16,256]{2,1,0:T(8,128)} %bitcast.26), calls=%async_computation.5 | async-start | bytes 2097152 | tf_op jit(solution)/shard_map/all_to_all | solution.py:90
  256.7 50.0 %all-to-all-done.5 = f32[64,16,256]{2,1,0:T(8,128)S(1)} async-done(((f32[64,16,256]{2,1,0:T(8,128)}), f32[64,16,256]{2,1,0:T(8,128)S(1)}, u32[]{:S(2)}, u32[]{:S(2)}) %all-to-all-start.5) | async-done | bytes 1048608 | tf_op jit(solution)/shard_map/all_to_all | solution.py:90
  306.7 4.0 tile.4
  310.7 10.5 %all-to-all-start = ((bf16[4,1024,512]{2,0,1:T(4,128)(2,1)}), bf16[4,1024,512]{2,0,1:T(4,128)(2,1)}, u32[]{:S(2)}, u32[]{:S(2)}) async-start(bf16[4,1024,512]{2,0,1:T(4,128)(2,1)} %bitcast.90), calls=%async_computation | async-start | bytes 8388608 | tf_op jit(solution)/shard_map/all_to_all | solution.py:11
  321.2 1.2 copy.91
  322.4 2.6 broadcast_multiply_fusion
  325.0 176.5 %all-to-all-done = bf16[4,1024,512]{2,0,1:T(4,128)(2,1)} async-done(((bf16[4,1024,512]{2,0,1:T(4,128)(2,1)}), bf16[4,1024,512]{2,0,1:T(4,128)(2,1)}, u32[]{:S(2)}, u32[]{:S(2)}) %all-to-all-start) | async-done | bytes 4194336 | tf_op jit(solution)/shard_map/all_to_all | solution.py:11
  501.6 12.8 %all-to-all-start.7 = ((f32[8,64,16,128]{3,1,2,0:T(8,128)}), f32[8,64,16,128]{3,1,2,0:T(8,128)}, u32[]{:S(2)}, u32[]{:S(2)}) async-start(f32[8,64,16,128]{3,1,2,0:T(8,128)} %broadcast_multiply_fusion), calls=%async_computation.7 | async-start | bytes 8388608 | tf_op jit(solution)/shard_map/all_to_all | solution.py:113
  514.5 4.4 constant_dynamic-slice_fusion.1
  520.6 1.9 copy.86
  522.5 39.1 %all-to-all-done.7 = f32[8,64,16,128]{3,1,2,0:T(8,128)} async-done(((f32[8,64,16,128]{3,1,2,0:T(8,128)}), f32[8,64,16,128]{3,1,2,0:T(8,128)}, u32[]{:S(2)}, u32[]{:S(2)}) %all-to-all-start.7) | async-done | bytes 4194336 | tf_op jit(solution)/shard_map/all_to_all | solution.py:113
  561.5 9.1 %all-to-all-start.4 = ((f32[64,16,512]{2,1,0:T(8,128)}), f32[64,16,512]{2,1,0:T(8,128)S(1)}, u32[]{:S(2)}, u32[]{:S(2)}) async-start(f32[64,16,512]{2,1,0:T(8,128)} %bitcast.92), calls=%async_computation.4 | async-start | bytes 4194304 | tf_op jit(solution)/shard_map/all_to_all | solution.py:83
  570.7 3.5 fusion.3
  574.2 2.5 copy.92
  576.7 1.7 convolution_convert_fusion.2
  578.4 1.1 copy.95
  581.0 80.5 %all-to-all-done.4 = f32[64,16,512]{2,1,0:T(8,128)S(1)} async-done(((f32[64,16,512]{2,1,0:T(8,128)}), f32[64,16,512]{2,1,0:T(8,128)S(1)}, u32[]{:S(2)}, u32[]{:S(2)}) %all-to-all-start.4) | async-done | bytes 2097184 | tf_op jit(solution)/shard_map/all_to_all | solution.py:83
  661.5 2.0 fusion
  663.5 60.9 %all-reduce.2 = (bf16[4,16,512]{2,0,1:T(4,128)(2,1)S(1)}, bf16[64,16,256]{2,0,1:T(8,128)(2,1)S(1)}) all-reduce(f32[4,16,512]{2,0,1:T(4,128)S(1)} %fusion, f32[64,16,256]{2,0,1:T(8,128)} %fusion.3), channel_id=1, replica_groups=mesh['grp'=8,'mem'=64] {'grp'}, use_global_device_ids=true, to_apply=%region_1.2 | all-reduce | flops 294912 | bytes 1769472 | tf_op jit(solution)/shard_map/psum | solution.py:100
  725.0 1.1 copy.94
  (51 shorter events, 8.6 us)
Async XLA Ops:
  0.6 105.5 %copy-start = (bf16[128,16,128]{2,1,0:T(8,128)(2,1)S(1)}, bf16[128,16,128]{2,1,0:T(8,128)(2,1)}, u32[]{:S(2)}) copy-start(bf16[128,16,128]{2,1,0:T(8,128)(2,1)} %param.11) | copy-start | bytes 1572868
  141.6 39.0 %copy-start.1 = (bf16[128,1024]{1,0:T(8,128)(2,1)S(1)}, bf16[128,1024]{1,0:T(8,128)(2,1)}, u32[]{:S(2)}) copy-start(bf16[128,1024]{1,0:T(8,128)(2,1)} %param.6) | copy-start | bytes 786436
  142.5 38.3 %copy-start.5 = (bf16[128,1024]{1,0:T(8,128)(2,1)S(1)}, bf16[128,1024]{1,0:T(8,128)(2,1)}, u32[]{:S(2)}) copy-start(bf16[128,1024]{1,0:T(8,128)(2,1)} %param.7) | copy-start | bytes 786436
  142.5 30.1 %all-to-all-start.3 = ((bf16[64,16,128]{2,1,0:T(8,128)(2,1)}), bf16[64,16,128]{2,1,0:T(8,128)(2,1)S(1)}, u32[]{:S(2)}, u32[]{:S(2)}) async-start(bf16[64,16,128]{2,1,0:T(8,128)(2,1)} %copy.85), calls=%async_computation.3 | async-start | bytes 524288 | tf_op jit(solution)/shard_map/all_to_all | solution.py:77
  172.6 36.3 %all-to-all-start.1 = ((bf16[64,16,256]{2,1,0:T(8,128)(2,1)}), bf16[64,16,256]{2,1,0:T(8,128)(2,1)S(1)}, u32[]{:S(2)}, u32[]{:S(2)}) async-start(bf16[64,16,256]{2,1,0:T(8,128)(2,1)} %copy.80), calls=%async_computation.1 | async-start | bytes 1048576 | tf_op jit(solution)/shard_map/all_to_all | solution.py:69
  208.9 10.9 %copy-start.6 = (bf16[64,16,256]{2,1,0:T(8,128)(2,1)}, bf16[64,16,256]{2,1,0:T(8,128)(2,1)S(1)}, u32[]{:S(2)}) copy-start(bf16[64,16,256]{2,1,0:T(8,128)(2,1)S(1)} %all-to-all-done.1) | copy-start | bytes 1572868
  208.9 38.8 %all-to-all-start.6 = ((f32[64,16,128]{2,1,0:T(8,128)}), f32[64,16,128]{2,1,0:T(8,128)}, u32[]{:S(2)}, u32[]{:S(2)}) async-start(f32[64,16,128]{2,1,0:T(8,128)} %bitcast.31), calls=%async_computation.6 | async-start | bytes 1048576 | tf_op jit(solution)/shard_map/all_to_all | solution.py:101
  219.8 36.8 %copy-start.8 = (bf16[4,16,512]{2,1,0:T(8,128)(2,1)S(1)}, bf16[4,16,512]{2,1,0:T(8,128)(2,1)}, u32[]{:S(2)}) copy-start(bf16[4,16,512]{2,1,0:T(8,128)(2,1)} %param.9) | copy-start | bytes 196612
  247.7 59.0 %all-to-all-start.5 = ((f32[64,16,256]{2,1,0:T(8,128)}), f32[64,16,256]{2,1,0:T(8,128)S(1)}, u32[]{:S(2)}, u32[]{:S(2)}) async-start(f32[64,16,256]{2,1,0:T(8,128)} %bitcast.26), calls=%async_computation.5 | async-start | bytes 2097152 | tf_op jit(solution)/shard_map/all_to_all | solution.py:90
  306.7 4.0 copy-start.2
  310.7 190.9 %all-to-all-start = ((bf16[4,1024,512]{2,0,1:T(4,128)(2,1)}), bf16[4,1024,512]{2,0,1:T(4,128)(2,1)}, u32[]{:S(2)}, u32[]{:S(2)}) async-start(bf16[4,1024,512]{2,0,1:T(4,128)(2,1)} %bitcast.90), calls=%async_computation | async-start | bytes 8388608 | tf_op jit(solution)/shard_map/all_to_all | solution.py:11
  325.0 189.3 %copy-start.9 = (s32[1,3]{1,0:T(1,128)S(1)}, s32[1,3]{1,0:T(1,128)}, u32[]{:S(2)}) copy-start(s32[1,3]{1,0:T(1,128)} %param.8) | copy-start | bytes 40
  501.6 60.0 %all-to-all-start.7 = ((f32[8,64,16,128]{3,1,2,0:T(8,128)}), f32[8,64,16,128]{3,1,2,0:T(8,128)}, u32[]{:S(2)}, u32[]{:S(2)}) async-start(f32[8,64,16,128]{3,1,2,0:T(8,128)} %broadcast_multiply_fusion), calls=%async_computation.7 | async-start | bytes 8388608 | tf_op jit(solution)/shard_map/all_to_all | solution.py:113
  519.1 1.0 copy-start.3
  561.5 100.0 %all-to-all-start.4 = ((f32[64,16,512]{2,1,0:T(8,128)}), f32[64,16,512]{2,1,0:T(8,128)S(1)}, u32[]{:S(2)}, u32[]{:S(2)}) async-start(f32[64,16,512]{2,1,0:T(8,128)} %bitcast.92), calls=%async_computation.4 | async-start | bytes 4194304 | tf_op jit(solution)/shard_map/all_to_all | solution.py:83
  576.7 2.8 copy-start.4
  578.4 1.5 copy-start.7
